TPU v7x, 256 devices: a whole 4x4x8 slice. The times are simulated.
256 devices in a mesh: seq: 16 (over y, x), head: 8 (over z), dp: 2 (over core).
Axes of the slice: x: 4, y: 4, z: 8, core: 2. Of those that a mesh axis runs over, the one named last changes fastest.
Arguments:
- hidden: bfloat16 [8192, 2560], P(('dp', 'seq', 'head')), parts along dimension 0, may hold values from -6 to 6
- x_input: bfloat16 [8192, 5120], P(('dp', 'seq', 'head')), parts along dimension 0, may hold values from -6 to 6
- grad_out: bfloat16 [8192, 5120], P(('dp', 'seq', 'head')), parts along dimension 0, may hold values from -6 to 6
- bc_weight: bfloat16 [2560, 256], replicated, may hold values from -0.01953125 to 0.01953125
- dt_weight: bfloat16 [2560, 80], replicated, may hold values from -0.125 to 0.125
- dt_bias: float32 [80], replicated, may hold values from -3 to -2
- a_log: float32 [80], replicated, may hold values from -10 to -1.6
- d_skip: float32 [80], replicated, may hold values from 0.5 to 1.5
Outputs:
- mixer_out: bfloat16 [8192, 5120], P(('dp', 'seq', 'head')), parts along dimension 0
- grad_x: bfloat16 [8192, 5120], P(('dp', 'seq', 'head')), parts along dimension 0
- grad_hidden: bfloat16 [8192, 2560], P(('dp', 'seq', 'head')), parts along dimension 0
- grad_bc_weight: float32 [5120, 256], P('dp'), parts along dimension 0
- grad_dt_weight: float32 [5120, 80], P('dp'), parts along dimension 0
- param_grads: float32 [6, 80], P('dp'), parts along dimension 0
There are 2 independent parts, one for each index of `dp`. A program takes and returns all parts, laid end to end along the dimension named above; an argument that names none is the same for every part. Nothing has to cross between parts.
All inputs are finite; a program needn't handle non-finite values.
Results may differ from a plain program's by a relative error of at most 0.02.
Values may be sent and summed in bfloat16 or wider, within the bound.
No kernel may reach another device: no remote copies, remote signals or barrier semaphores. Data moves between devices by JAX's collectives and lax.ppermute only.
A program may use at most 128 MiB of HBM per device.

v0:
```python
import jax
import jax.numpy as jnp
from jax import lax
from jax.sharding import PartitionSpec as P

Q = 256
precise = lax.Precision.HIGHEST


def prefix_2(value, axis, combine, identity):
    devices, place = (lax.axis_size(axis), lax.axis_index(axis))
    everything = jax.tree.map(
        lambda part, kind: lax.all_gather(part.astype(kind), axis),
        value,
        (jnp.bfloat16, jnp.bfloat16),
    )
    start = jax.tree.map(
        lambda part, zero: jnp.broadcast_to(jnp.asarray(zero, part.dtype), part.shape),
        value,
        identity,
    )

    def step(k, before):
        reached = k < place
        new = combine(
            before, jax.tree.map(lambda part, own: part[k].astype(own.dtype), everything, value)
        )
        return jax.tree.map(lambda a, b: jnp.where(reached, a, b), new, before)

    return lax.fori_loop(0, devices, step, start)


def prefix_3(part, axis, combine, identity):
    count = lax.axis_size(axis)
    place = lax.axis_index(axis)
    ahead = count - 1 - place
    gathered = jax.tree.map(lambda a: lax.all_gather(a, axis), part)
    state = jax.tree.map(lambda a, e: jnp.zeros_like(a) + jnp.asarray(e, a.dtype), part, identity)

    def one(step, state):
        source = count - 1 - step
        return combine(
            state, jax.tree.map(lambda a: lax.dynamic_index_in_dim(a, source, 0, False), gathered)
        )

    return lax.fori_loop(0, ahead, one, state)


def span_scan(x_heads, step_size, b_rows, c_rows, neg_rate, state_in):
    length = x_heads.shape[0]
    blocks = length // Q
    heads_here = x_heads.shape[1]
    head_width = x_heads.shape[2]
    states = b_rows.shape[1]
    causal = (jnp.arange(Q)[:, None] >= jnp.arange(Q)[None, :])[:, :, None]

    def span_advance(carry, block):
        x_block, step_block, b_block, c_block = block
        running = jnp.cumsum(step_block * neg_rate[None, :], axis=0)
        scores = jnp.dot(c_block, b_block.T, precision=precise)
        spread = running[:, None, :] - running[None, :, :]
        decay = jnp.where(causal, jnp.exp(jnp.where(causal, spread, 0.0)), 0.0)
        scaled_x = x_block * step_block[:, :, None]
        inner = jnp.einsum("qkh,khp->qhp", decay * scores[:, :, None], scaled_x, precision=precise)
        carried = (
            jnp.einsum("qn,hnp->qhp", c_block, carry, precision=precise)
            * jnp.exp(running)[:, :, None]
        )
        total = running[-1]
        weights_end = jnp.exp(total[None, :] - running)
        fresh = jnp.einsum(
            "kn,khp->hnp", b_block, scaled_x * weights_end[:, :, None], precision=precise
        )
        return (jnp.exp(total)[:, None, None] * carry + fresh, inner + carried)

    pieces = (
        x_heads.reshape(blocks, Q, heads_here, head_width),
        step_size.reshape(blocks, Q, heads_here),
        b_rows.reshape(blocks, Q, states),
        c_rows.reshape(blocks, Q, states),
    )
    state_out, outputs = lax.scan(jax.checkpoint(span_advance), state_in, pieces)
    return (outputs.reshape(length, heads_here, head_width), state_out)


def mixer_local(x_heads, raw_step, b_rows, c_rows, log_decay, skip_gain, step_bias, state_in):
    step_size = jax.nn.softplus(raw_step + step_bias[None, :])
    neg_rate = -jnp.exp(log_decay)
    mixed, state_out = span_scan(x_heads, step_size, b_rows, c_rows, neg_rate, state_in)
    return (mixed + skip_gain[None, :, None] * x_heads, state_out)


def device_totals(x_heads, step_size, b_rows, c_rows, grad_heads, neg_rate):
    length = x_heads.shape[0]
    heads_here = x_heads.shape[1]
    head_width = x_heads.shape[2]
    states = b_rows.shape[1]
    blocks = length // Q

    def device_advance(carry, block):
        prefix, state_sum, adjoint_sum = carry
        x_block, step_block, b_block, c_block, grad_block = block
        running = jnp.cumsum(step_block * neg_rate[None, :], axis=0)
        total = running[-1]
        weights_end = jnp.exp(total[None, :] - running)
        scaled_x = x_block * step_block[:, :, None]
        fresh = jnp.einsum(
            "kn,khp->hnp", b_block, scaled_x * weights_end[:, :, None], precision=precise
        )
        state_sum = jnp.exp(total)[:, None, None] * state_sum + fresh
        reach = jnp.exp(prefix[None, :] + running)
        adjoint_sum = adjoint_sum + jnp.einsum(
            "qn,qhp->hnp", c_block, grad_block * reach[:, :, None], precision=precise
        )
        return ((prefix + total, state_sum, adjoint_sum), None)

    pieces = (
        x_heads.reshape(blocks, Q, heads_here, head_width),
        step_size.reshape(blocks, Q, heads_here),
        b_rows.reshape(blocks, Q, states),
        c_rows.reshape(blocks, Q, states),
        grad_heads.reshape(blocks, Q, heads_here, head_width),
    )
    start = (
        jnp.zeros((heads_here,), jnp.float32),
        jnp.zeros((heads_here, states, head_width), jnp.float32),
        jnp.zeros((heads_here, states, head_width), jnp.float32),
    )
    (prefix, state_sum, adjoint_sum), unused = lax.scan(device_advance, start, pieces)
    return (jnp.exp(prefix), state_sum, adjoint_sum)


def combine_pairs(earlier, later):
    return (earlier[0] * later[0], later[0][:, None, None] * earlier[1] + later[1])


def per_device(hidden, x_input, grad_out, bc_weight, dt_weight, dt_bias, a_log, d_skip):
    groups = lax.axis_size("head")
    head_index = lax.axis_index("head")
    heads_all = dt_weight.shape[1]
    heads_local = heads_all // groups
    head_width = x_input.shape[1] // heads_all
    states = bc_weight.shape[1] // 2
    proj_bc = jnp.dot(hidden, bc_weight, preferred_element_type=jnp.float32).astype(jnp.bfloat16)
    proj_dt = jnp.dot(hidden, dt_weight, preferred_element_type=jnp.float32).astype(jnp.bfloat16)
    x_local, raw_local, grad_local = (
        lax.all_to_all(x_input, "head", split_axis=1, concat_axis=0, tiled=True),
        lax.all_to_all(proj_dt, "head", split_axis=1, concat_axis=0, tiled=True),
        lax.all_to_all(grad_out, "head", split_axis=1, concat_axis=0, tiled=True),
    )
    bc_local = lax.all_gather(proj_bc, "head", axis=0, tiled=True)
    length = x_local.shape[0]
    x_heads = x_local.astype(jnp.float32).reshape(length, heads_local, head_width)
    grad_heads = grad_local.astype(jnp.float32).reshape(length, heads_local, head_width)
    raw_step = raw_local.astype(jnp.float32)
    b_rows = bc_local[:, :states].astype(jnp.float32)
    c_rows = bc_local[:, states:].astype(jnp.float32)
    offset = head_index * heads_local
    bias_local = lax.dynamic_slice_in_dim(dt_bias, offset, heads_local)
    log_local = lax.dynamic_slice_in_dim(a_log, offset, heads_local)
    skip_local = lax.dynamic_slice_in_dim(d_skip, offset, heads_local)
    step_size = jax.nn.softplus(raw_step + bias_local[None, :])
    neg_rate = -jnp.exp(log_local)
    decay_all, state_sum, adjoint_sum = device_totals(
        x_heads, step_size, b_rows, c_rows, grad_heads, neg_rate
    )
    identity = (
        jnp.ones((heads_local,), jnp.float32),
        jnp.zeros((heads_local, states, head_width), jnp.float32),
    )
    state_in = prefix_2((decay_all, state_sum), "seq", combine_pairs, identity)[1]
    state_grad = prefix_3((decay_all, adjoint_sum), "seq", combine_pairs, identity)[1]

    def forward(x_arg, raw_arg, b_arg, c_arg, log_arg, skip_arg, bias_arg):
        return mixer_local(x_arg, raw_arg, b_arg, c_arg, log_arg, skip_arg, bias_arg, state_in)

    (mixed, state_end), pullback = jax.vjp(
        forward, x_heads, raw_step, b_rows, c_rows, log_local, skip_local, bias_local
    )
    grad_xs, grad_raw, grad_b, grad_c, grad_alog, grad_skip, grad_bias = pullback(
        (grad_heads, state_grad)
    )
    out_local = mixed.reshape(length, heads_local * head_width).astype(jnp.bfloat16)
    gradx_local = grad_xs.reshape(length, heads_local * head_width).astype(jnp.bfloat16)
    step_local = grad_raw.astype(jnp.bfloat16)
    mixer_out, grad_x, d_step = (
        lax.all_to_all(out_local, "head", split_axis=0, concat_axis=1, tiled=True),
        lax.all_to_all(gradx_local, "head", split_axis=0, concat_axis=1, tiled=True),
        lax.all_to_all(step_local, "head", split_axis=0, concat_axis=1, tiled=True),
    )
    d_bc = lax.psum_scatter(
        jnp.concatenate([grad_b, grad_c], axis=1).astype(jnp.bfloat16),
        "head",
        scatter_dimension=0,
        tiled=True,
    )
    grad_hidden = (
        jnp.dot(d_bc, bc_weight.T, preferred_element_type=jnp.float32)
        + jnp.dot(d_step, dt_weight.T, preferred_element_type=jnp.float32)
    ).astype(jnp.bfloat16)
    seq_total = length * lax.axis_size("seq")
    weight_bc = jnp.dot(hidden.T, d_bc, preferred_element_type=jnp.float32) / seq_total
    weight_dt = jnp.dot(hidden.T, d_step, preferred_element_type=jnp.float32) / seq_total
    stacked = jnp.stack([grad_bias, grad_alog, grad_skip]) / seq_total
    param_local = lax.dynamic_update_slice(
        jnp.zeros((3, heads_all), jnp.float32), stacked, (0, offset)
    )
    grad_bc_weight, grad_dt_weight, param_grads = lax.psum(
        (weight_bc, weight_dt, param_local), ("seq", "head")
    )
    return (mixer_out, grad_x, grad_hidden, grad_bc_weight, grad_dt_weight, param_grads)


def solution(mesh):
    in_specs = (
        P(("dp", "seq", "head"), None),
        P(("dp", "seq", "head"), None),
        P(("dp", "seq", "head"), None),
        P(),
        P(),
        P(),
        P(),
        P(),
    )
    out_specs = (
        P(("dp", "seq", "head"), None),
        P(("dp", "seq", "head"), None),
        P(("dp", "seq", "head"), None),
        P("dp", None),
        P("dp", None),
        P("dp", None),
    )
    return jax.shard_map(
        per_device, mesh=mesh, in_specs=in_specs, out_specs=out_specs, check_vma=False
    )
```

profile of v0, /device:TPU:0, one launch (start us, length us, event | category | flops | bytes accessed | tf_op | source)
XLA Modules:
  0.0 757.0 jit_solution(9546356608684292287)
XLA Ops:
  7.2 1.4 convolution_convert_fusion.1
  9.5 6.7 all-to-all-start.1
  18.2 1.7 copy.316
  19.9 4.0 all-to-all-done.1
  23.9 3.4 all-to-all-start
  27.4 27.6 %all_gather.23 = bf16[256,256]{1,0:T(8,128)(2,1)S(1)} all-gather(bf16[32,256]{1,0:T(8,128)(2,1)S(1)} %convolution_convert_fusion), channel_id=1, replica_groups=mesh['seq'=16,'head'=8,'dp'=2] {'head'}, dimensions={0}, use_global_device_ids=true | all-gather | bytes 147456 | tf_op jit(solution)/shard_map/all_gather | solution.py:151
  57.0 6.1 all-to-all-start.3
  66.0 1.5 mul.420.clone
  68.8 1.5 copy.234
  70.3 1.5 mul.416
  73.8 1.5 mul.406
  77.8 3.5 multiply_reduce_fusion
  81.3 1.5 mul.419
  82.8 2.6 fusion.62
  85.5 1.5 mul.429
  87.1 2.0 fusion.56
  91.4 20.9 %all-gather.2 = bf16[16,1,10]{2,1,0:T(2,128)(2,1)S(1)} all-gather(bf16[1,1,10]{2,1,0:T(2,128)(2,1)S(1)} %bitcast.278), channel_id=1, replica_groups=mesh['seq'=16,'head'=8,'dp'=2] {'seq'}, dimensions={0}, use_global_device_ids=true | all-gather | bytes 340 | tf_op jit(solution)/shard_map/all_gather | solution.py:13
  112.3 21.2 %all-gather.3 = f32[16,1,10]{2,1,0:T(1,128)} all-gather(f32[1,1,10]{2,1,0:T(1,128)} %bitcast.276), channel_id=1, replica_groups=mesh['seq'=16,'head'=8,'dp'=2] {'seq'}, dimensions={0}, use_global_device_ids=true | all-gather | bytes 680 | tf_op jit(solution)/shard_map/all_gather | solution.py:37
  134.5 1.8 reshape.371
  137.4 1.8 reshape.373
  139.1 22.0 %while.21 = (s32[]{:T(128)}, f32[10,128,64]{2,1,0:T(8,128)S(1)}, s32[]{:T(128)}, bf16[16,10]{1,0:T(8,128)(2,1)S(1)}, bf16[16,10,128,64]{2,3,1,0:T(8,128)(2,1)}, /*index=5*/s32[]{:T(128)}, s32[]{:T(128)}) while((s32[]{:T(128)}, f32[10,128,64]{2,1,0:T(8,128)S(1)}, s32[]{:T(128)}, bf16[16,10]{1,0:T(8,128)(2,1)S(1)}, ...), condition=%wide.region_3.4_spmd.clone, body=%wide.region_2.3_spmd.clone.sunk | while | flops 409614 | bytes 1474765 | solution.py:30
  161.1 41.3 %all-gather.9.cloned.1.call-done = f32[160,128,64]{1,2,0:T(8,128)} async-done(((f32[10,128,64]{1,2,0:T(8,128)}), f32[160,128,64]{1,2,0:T(8,128)}) %all-gather.9.cloned.1.call-update) | async-done | bytes 5242896 | tf_op jit(solution)/shard_map/all_gather | solution.py:37
  202.5 57.5 %while.20 = (s32[]{:T(128)}, f32[10,128,64]{2,1,0:T(8,128)S(1)}, s32[]{:T(128)}, f32[16,10]{1,0:T(8,128)}, f32[16,10,128,64]{2,3,1,0:T(8,128)}, /*index=5*/s32[]{:T(128)}, s32[]{:T(128)}, s32[]{:T(128)}, s32[]{:T(128)}) while((s32[]{:T(128)}, f32[10,128,64]{2,1,0:T(8,128)S(1)}, s32[]{:T(128)}, f32[16,10]{1,0:T(8,128)}, ...), condition=%wide.region_5.6_spmd, body=%wide.region_4.5_spmd.sunk | while | flops 163846 | bytes 2294027 | solution.py:46
  202.5 1.7 constant_dynamic-slice_fusion.4
  206.4 1.7 constant_dynamic-slice_fusion.4
  210.2 1.7 constant_dynamic-slice_fusion.4
  214.0 1.7 constant_dynamic-slice_fusion.4
  217.8 1.7 constant_dynamic-slice_fusion.4
  221.6 1.7 constant_dynamic-slice_fusion.4
  225.4 1.7 constant_dynamic-slice_fusion.4
  229.3 1.7 constant_dynamic-slice_fusion.4
  233.1 1.7 constant_dynamic-slice_fusion.4
  236.9 1.7 constant_dynamic-slice_fusion.4
  240.7 1.7 constant_dynamic-slice_fusion.4
  244.5 1.7 constant_dynamic-slice_fusion.4
  248.4 1.7 constant_dynamic-slice_fusion.4
  252.2 1.7 constant_dynamic-slice_fusion.4
  256.0 1.7 constant_dynamic-slice_fusion.4
  264.8 2.1 fusion.71
  268.0 3.0 copy.262
  271.0 3.0 copy.251
  274.0 2.2 copy.254
  276.2 2.1 convolution_bitcast_fusion
  278.4 5.8 fusion.19
  284.3 3.9 multiply_reduce_fusion.3
  289.7 1.7 fusion.118
  293.2 2.7 reduce-window.42
  296.2 2.3 broadcast_multiply_fusion
  298.5 1.7 fusion.65
  302.8 7.0 all-to-all-start.5
  310.7 6.8 all-to-all-done.5
  318.8 28.1 %reduce-scatter.4.cloned.1.call-done = bf16[32,256]{1,0:T(8,128)(2,1)} async-done(((bf16[256,256]{1,0:T(8,128)(2,1)}), bf16[32,256]{1,0:T(8,128)(2,1)}) %reduce-scatter.4.cloned.1.call-update) | async-done | bytes 16400
  346.9 2.7 fusion.1
  350.5 3.6 broadcast_multiply_fusion.1
  354.8 6.0 fusion.48
  360.9 2.4 copy.238
  364.6 2.4 copy.252
  367.0 1.3 reshape.363
  368.3 2.6 add_convert_fusion
  370.9 4.4 all-to-all-start.2
  375.6 14.4 %all-to-all-done.2 = bf16[8,32,640]{2,1,0:T(8,128)(2,1)S(1)} async-done(((bf16[8,32,640]{2,1,0:T(8,128)(2,1)}), bf16[8,32,640]{2,1,0:T(8,128)(2,1)S(1)}, u32[]{:S(2)}, u32[]{:S(2)}) %all-to-all-start.2) | async-done | bytes 327712 | tf_op jit(solution)/shard_map/all_to_all | solution.py:187
  390.0 3.4 all-to-all-start.4
  393.6 349.3 %psum.23 = f32[3,80]{1,0:T(4,128)} all-reduce(f32[3,80]{1,0:T(4,128)S(1)} %dynamic_update_slice.19), channel_id=1, replica_groups=mesh['seq'=16,'head'=8,'dp'=2] {'seq','head'}, use_global_device_ids=true, to_apply=%region_25.26 | all-reduce | flops 240 | bytes 1920 | tf_op jit(solution)/shard_map/psum | solution.py:208
  745.9 3.3 copy.269
  (317 shorter events, 91.2 us)
Async XLA Ops:
  7.2 9.0 %copy-start = (bf16[2560,256]{1,0:T(8,128)(2,1)S(1)}, bf16[2560,256]{1,0:T(8,128)(2,1)}, u32[]{:S(2)}) copy-start(bf16[2560,256]{1,0:T(8,128)(2,1)} %param.15) | copy-start | bytes 3932164
  7.2 47.8 %copy-start.45 = (f32[80]{0:T(128)S(1)}, f32[80]{0:T(128)}, u32[]{:S(2)}) copy-start(f32[80]{0:T(128)} %param.17) | copy-start | bytes 964
  7.2 47.9 %copy-start.14 = (bf16[32,5120]{1,0:T(8,128)(2,1)S(1)}, bf16[32,5120]{1,0:T(8,128)(2,1)}, u32[]{:S(2)}) copy-start(bf16[32,5120]{1,0:T(8,128)(2,1)} %param.14) | copy-start | bytes 983044
  9.5 14.5 %all-to-all-start.1 = ((bf16[8,2,160]{2,1,0:T(2,128)(2,1)}), bf16[8,2,160]{2,1,0:T(2,128)(2,1)S(1)}, u32[]{:S(2)}, u32[]{:S(2)}) async-start(bf16[8,2,160]{2,1,0:T(2,128)(2,1)} %reshape.399), calls=%async_computation.1 | async-start | bytes 16384 | tf_op jit(solution)/shard_map/all_to_all | solution.py:148
  18.2 46.4 %copy-start.34 = (f32[10]{0:T(128)}, f32[10]{0:T(128)S(1)}, u32[]{:S(2)}) copy-start(f32[10]{0:T(128)S(1)} %fusion.113) | copy-start | bytes 124
  23.9 33.0 %all-to-all-start = ((bf16[32,8,640]{2,0,1:T(8,128)(2,1)}), bf16[32,8,640]{2,0,1:T(8,128)(2,1)S(1)}, u32[]{:S(2)}, u32[]{:S(2)}) async-start(bf16[32,8,640]{2,0,1:T(8,128)(2,1)} %bitcast.236), calls=%async_computation | async-start | bytes 655360 | tf_op jit(solution)/shard_map/all_to_all | solution.py:147
  55.1 9.6 %copy-start.36 = (f32[10]{0:T(128)}, f32[10]{0:T(128)S(1)}, u32[]{:S(2)}) copy-start(f32[10]{0:T(128)S(1)} %dynamic_slice.73) | copy-start | bytes 124
  55.9 8.7 %copy-start.15 = (bf16[8,10,32]{2,1,0:T(8,128)(2,1)}, bf16[8,10,32]{2,1,0:T(8,128)(2,1)S(1)}, u32[]{:S(2)}) copy-start(bf16[8,10,32]{2,1,0:T(8,128)(2,1)S(1)} %reshape.400) | copy-start | bytes 15364
  56.0 7.1 copy-start.22
  57.0 7.7 %copy-start.1 = (bf16[32,8,640]{2,0,1:T(8,128)(2,1)}, bf16[32,8,640]{2,0,1:T(8,128)(2,1)S(1)}, u32[]{:S(2)}) copy-start(bf16[32,8,640]{2,0,1:T(8,128)(2,1)S(1)} %all-to-all-done) | copy-start | bytes 983044
  57.0 20.9 %all-to-all-start.3 = ((bf16[32,8,640]{2,0,1:T(8,128)(2,1)}), bf16[32,8,640]{2,0,1:T(8,128)(2,1)}, u32[]{:S(2)}, u32[]{:S(2)}) async-start(bf16[32,8,640]{2,0,1:T(8,128)(2,1)} %bitcast.235), calls=%async_computation.3 | async-start | bytes 655360 | tf_op jit(solution)/shard_map/all_to_all | solution.py:149
  63.0 76.1 %all-gather.7.cloned.1.call-start = ((), (), s32[]{:S(2)}) async-start(), calls=%async_computation.7 | async-start | bytes 2785280 | tf_op jit(solution)/shard_map/all_gather | solution.py:13
  63.2 1.4 copy-start.20
  63.9 0.7 copy-start.41
  64.6 0.6 copy-start.26
  85.5 117.0 %all-gather.9.cloned.1.call-start = ((), (), s32[]{:S(2)}) async-start(), calls=%async_computation.8 | async-start | bytes 5570560 | tf_op jit(solution)/shard_map/all_gather | solution.py:37
  90.5 176.4 %copy-start.3 = (f32[256,128]{1,0:T(8,128)}, f32[256,128]{1,0:T(8,128)S(1)}, u32[]{:S(2)}) copy-start(f32[256,128]{1,0:T(8,128)S(1)} %get-tuple-element.368) | copy-start | bytes 393220
  260.0 4.9 copy-start.5
  261.7 9.3 %copy-start.38 = (f32[10]{0:T(128)}, f32[10]{0:T(128)S(1)}, u32[]{:S(2)}) copy-start(f32[10]{0:T(128)S(1)} %slice_bitcast_fusion) | copy-start | bytes 124
  278.4 5.8 copy-start.11
  278.4 5.8 copy-start.12
  278.4 5.8 copy-start.17
  278.4 5.8 copy-start.25
  278.4 5.8 copy-start.28
  278.4 5.8 copy-start.32
  288.1 4.6 copy-start.31
  288.1 4.7 copy-start.30
  288.1 4.9 copy-start.43
  288.1 4.9 copy-start.39
  296.1 4.1 copy-start.4
  296.1 4.1 copy-start.9
  296.2 4.1 copy-start.13
  296.2 4.5 copy-start.6
  298.4 2.6 copy-start.23
  298.4 2.6 copy-start.33
  298.5 2.6 copy-start.35
  298.5 2.6 copy-start.37
  298.5 3.5 copy-start.16
  298.5 19.2 %copy-start.2 = (bf16[32,2560]{1,0:T(8,128)(2,1)S(1)}, bf16[32,2560]{1,0:T(8,128)(2,1)}, u32[]{:S(2)}) copy-start(bf16[32,2560]{1,0:T(8,128)(2,1)} %param.12) | copy-start | bytes 491524
  302.8 14.7 %all-to-all-start.5 = ((bf16[8,2,160]{2,1,0:T(2,128)(2,1)}), bf16[8,2,160]{2,1,0:T(2,128)(2,1)S(1)}, u32[]{:S(2)}, u32[]{:S(2)}) async-start(bf16[8,2,160]{2,1,0:T(2,128)(2,1)} %reshape.401), calls=%async_computation.5 | async-start | bytes 16384 | tf_op jit(solution)/shard_map/all_to_all | solution.py:189
  309.8 37.1 %reduce-scatter.4.cloned.1.call-start = ((), (), s32[]{:S(2)}) async-start(), calls=%async_computation.9 | async-start | bytes 147456
  310.7 435.2 %all-reduce.4.cloned.1.call-start = ((), (), s32[]{:S(2)}) async-start(), calls=%async_computation.10 | async-start | bytes 6881280 | tf_op jit(solution)/shard_map/psum | solution.py:208
  317.7 32.0 %copy-start.18 = (bf16[32,80]{0,1:T(8,128)(2,1)}, bf16[32,80]{0,1:T(8,128)(2,1)S(1)}, u32[]{:S(2)}) copy-start(bf16[32,80]{0,1:T(8,128)(2,1)S(1)} %all_to_all.80) | copy-start | bytes 15364
  318.8 30.8 %copy-start.46 = (f32[80]{0:T(128)S(1)}, f32[80]{0:T(128)}, u32[]{:S(2)}) copy-start(f32[80]{0:T(128)} %param.19) | copy-start | bytes 964
  349.6 0.9 copy-start.8
  350.5 4.3 copy-start.21
  350.5 4.3 copy-start.27
  366.9 8.3 %copy-start.29 = (f32[640]{0:T(1024)S(1)}, f32[640]{0:T(1024)}, u32[]{:S(2)}) copy-start(f32[640]{0:T(1024)} %get-tuple-element.533) | copy-start | bytes 7684
  367.0 8.5 %copy-start.42 = (f32[10]{0:T(128)S(1)}, f32[10]{0:T(128)}, u32[]{:S(2)}) copy-start(f32[10]{0:T(128)} %get-tuple-element.542) | copy-start | bytes 124
  367.0 8.5 %copy-start.44 = (f32[80]{0:T(128)S(1)}, f32[80]{0:T(128)}, u32[]{:S(2)}) copy-start(f32[80]{0:T(128)} %param.18) | copy-start | bytes 964
  368.3 25.2 %copy-start.40 = (f32[10]{0:T(128)S(1)}, f32[10]{0:T(128)}, u32[]{:S(2)}) copy-start(f32[10]{0:T(128)} %get-tuple-element.530) | copy-start | bytes 124
  368.3 374.6 %copy-start.24 = (bf16[32,256]{1,0:T(8,128)(2,1)S(1)}, bf16[32,256]{1,0:T(8,128)(2,1)}, u32[]{:S(2)}) copy-start(bf16[32,256]{1,0:T(8,128)(2,1)} %reduce-scatter.4.cloned.1.call-done) | copy-start | bytes 49156
  368.3 375.1 %copy-start.7 = (bf16[2560,80]{0,1:T(8,128)(2,1)S(1)}, bf16[2560,80]{0,1:T(8,128)(2,1)}, u32[]{:S(2)}) copy-start(bf16[2560,80]{0,1:T(8,128)(2,1)} %param.16) | copy-start | bytes 1228804
  368.3 375.1 %copy-start.19 = (bf16[32,80]{0,1:T(8,128)(2,1)S(1)}, bf16[32,80]{0,1:T(8,128)(2,1)}, u32[]{:S(2)}) copy-start(bf16[32,80]{0,1:T(8,128)(2,1)} %copy-done.18) | copy-start | bytes 15364
  370.9 19.1 %all-to-all-start.2 = ((bf16[8,32,640]{2,1,0:T(8,128)(2,1)}), bf16[8,32,640]{2,1,0:T(8,128)(2,1)S(1)}, u32[]{:S(2)}, u32[]{:S(2)}) async-start(bf16[8,32,640]{2,1,0:T(8,128)(2,1)} %get-tuple-element.546), calls=%async_computation.2 | async-start | bytes 655360 | tf_op jit(solution)/shard_map/all_to_all | solution.py:187
  390.0 355.1 %all-to-all-start.4 = ((bf16[8,32,640]{2,1,0:T(8,128)(2,1)}), bf16[8,32,640]{2,1,0:T(8,128)(2,1)S(1)}, u32[]{:S(2)}, u32[]{:S(2)}) async-start(bf16[8,32,640]{2,1,0:T(8,128)(2,1)} %get-tuple-element.545), calls=%async_computation.4 | async-start | bytes 655360 | tf_op jit(solution)/shard_map/all_to_all | solution.py:188
  745.9 3.3 copy-start.10
Sparse Core Ops, SparseCore 0:
  85.6 52.9 all-gather.6
  141.6 60.7 all-gather.8
  313.7 33.1 reduce-scatter.3
  353.9 237.4 all-reduce.3
where the time goes:
time: 768 us; the launch traced here: 757 us
  blocking collectives  419 us (55%)
  local copies, waits for them, and re-layouts  124 us (16%)
  waiting for transfers between devices  94.7 us (12%)
  matrix products  38.5 us (5%)
  other arithmetic  32.8 us (4%)
  starting transfers between devices  31.3 us (4%)
  between operations  14.9 us (2%)
    psum x1, blocking collectives, per_device(): lax.psum((weight_bc, weight_dt, param_local), ('seq', 'head'))  349 us
    dynamic_slice x30, local copies, waits for them, and re-layouts, one(): lax.dynamic_index_in_dim(a, source, 0, False)  44 us
    all_gather x1, waiting for transfers between devices, prefix_3(): gathered = jax.tree.map(lambda a: lax.all_gather(a, axis), part)  41.3 us
    unnamed x5, waiting for transfers between devices  28.1 us
    all_gather x1, blocking collectives, per_device(): bc_local = lax.all_gather(proj_bc, 'head', axis=0, tiled=True)  27.6 us
    all_gather x1, blocking collectives, prefix_3(): gathered = jax.tree.map(lambda a: lax.all_gather(a, axis), part)  21.2 us
    all_gather x1, blocking collectives, prefix_2(): lax.all_gather(part.astype(kind), axis)  20.9 us
    dynamic_slice x32, local copies, waits for them, and re-layouts, step(): part[k].astype(own.dtype)  18.6 us
  transfers between devices with their start and end apart: 10, of which 5 were waited for; matrix products, arithmetic and copies ran while one was open for 10% of the time, Pallas kernels for 0%

commit v1 on v0

--- a/solution.py
+++ b/solution.py
@@ -5,6 +5,17 @@
 
 Q = 256
 precise = lax.Precision.HIGHEST
+
+
+def around_the_ring(shard, mesh_axis, along):
+    count = lax.axis_size(mesh_axis)
+    route = [(i, (i + 1) % count) for i in range(count)]
+    terms = [shard]
+    for stride in range(1, count):
+        terms = [lax.ppermute(terms[0], mesh_axis, route), *terms]
+    whole = jnp.concatenate(terms, axis=along)
+    offset = (lax.axis_index(mesh_axis) + 1) * terms[-1].shape[along]
+    return jnp.roll(whole, offset, axis=along)
 
 
 def prefix_2(value, axis, combine, identity):
@@ -148,7 +159,7 @@
         lax.all_to_all(proj_dt, "head", split_axis=1, concat_axis=0, tiled=True),
         lax.all_to_all(grad_out, "head", split_axis=1, concat_axis=0, tiled=True),
     )
-    bc_local = lax.all_gather(proj_bc, "head", axis=0, tiled=True)
+    bc_local = around_the_ring(proj_bc, "head", 0)
     length = x_local.shape[0]
     x_heads = x_local.astype(jnp.float32).reshape(length, heads_local, head_width)
     grad_heads = grad_local.astype(jnp.float32).reshape(length, heads_local, head_width)

time: 768 us -> 777 us (1.012)
  blocking collectives: 419 us -> 392 us
  starting transfers between devices: 31.3 us -> 48.9 us
  waiting for transfers between devices: 94.7 us -> 106 us
    all_gather x1 -> x0, blocking collectives: 27.6 us -> none  [per_device(): bc_local = lax.all_gather(proj_bc, 'head', axis=0, tiled=True)]
    ppermute x0 -> x7, waiting for transfers between devices: none -> 23.6 us  [around_the_ring(): terms = [lax.ppermute(terms[0], mesh_axis, route), *terms]]
    all_gather x1, waiting for transfers between devices: 41.3 us -> 25.6 us  [prefix_3(): gathered = jax.tree.map(lambda a: lax.all_gather(a, axis), part)]
    all_gather x1, starting transfers between devices: 0.04 us -> 11 us  [prefix_3(): gathered = jax.tree.map(lambda a: lax.all_gather(a, axis), part)]
    unnamed x107 -> x132, local copies, waits for them, and re-layouts: 8.48 us -> 18.1 us
  transfers between devices with their start and end apart: 10 -> 17, of which waited for: 5 -> 11; matrix products, arithmetic and copies ran while one was open for 10% -> 11% of each run, Pallas kernels for 0% -> 0%
where the time goes in v1:
time: 777 us; the launch traced here: 764 us
  blocking collectives  392 us (50%)
  local copies, waits for them, and re-layouts  131 us (17%)
  waiting for transfers between devices  106 us (14%)
  starting transfers between devices  48.9 us (6%)
  matrix products  39.5 us (5%)
  other arithmetic  30.1 us (4%)
  between operations  14.9 us (2%)
    psum x1, blocking collectives, per_device(): lax.psum((weight_bc, weight_dt, param_local), ('seq', 'head'))  350 us
    dynamic_slice x30, local copies, waits for them, and re-layouts, one(): lax.dynamic_index_in_dim(a, source, 0, False)  44 us
    unnamed x5, waiting for transfers between devices  28.1 us
    all_gather x1, waiting for transfers between devices, prefix_3(): gathered = jax.tree.map(lambda a: lax.all_gather(a, axis), part)  25.6 us
    ppermute x7, waiting for transfers between devices, around_the_ring(): terms = [lax.ppermute(terms[0], mesh_axis, route), *terms]  23.6 us
    all_gather x1, blocking collectives, prefix_3(): gathered = jax.tree.map(lambda a: lax.all_gather(a, axis), part)  21.2 us
    all_gather x1, blocking collectives, prefix_2(): lax.all_gather(part.astype(kind), axis)  20.9 us
    dynamic_slice x32, local copies, waits for them, and re-layouts, step(): part[k].astype(own.dtype)  18.6 us
  transfers between devices with their start and end apart: 17, of which 11 were waited for; matrix products, arithmetic and copies ran while one was open for 11% of the time, Pallas kernels for 0%

profile of v1, /device:TPU:0, one launch (start us, length us, event | category | flops | bytes accessed | tf_op | source)
XLA Modules:
  0.0 763.8 jit_solution(8158561481899301002)
XLA Ops:
  9.5 6.7 all-to-all-start.1
  17.5 2.1 collective-permute-start
  21.0 1.7 copy.316
  24.0 5.3 all-to-all-start
  29.5 2.1 collective-permute-start.1
  32.3 5.4 collective-permute-done.1
  37.9 4.7 collective-permute-done.2
  42.8 4.8 collective-permute-done.3
  48.4 4.2 collective-permute-done.4
  53.3 4.4 collective-permute-done.5
  72.2 6.7 all-to-all-start.3
  83.3 6.8 all-to-all-done.3
  90.1 3.5 multiply_reduce_fusion
  95.2 2.8 fusion.62
  98.0 11.0 %all-gather.9.cloned.1.call-start = ((), (), s32[]{:S(2)}) async-start(), calls=%async_computation.8 | async-start | bytes 5570560 | tf_op jit(solution)/shard_map/all_gather | solution.py:48
  109.0 1.5 mul.433
  110.6 2.9 fusion.56
  114.3 20.9 %all-gather.2 = bf16[16,1,10]{2,1,0:T(2,128)(2,1)S(1)} all-gather(bf16[1,1,10]{2,1,0:T(2,128)(2,1)S(1)} %bitcast.279), channel_id=1, replica_groups=mesh['seq'=16,'head'=8,'dp'=2] {'seq'}, dimensions={0}, use_global_device_ids=true | all-gather | bytes 340 | tf_op jit(solution)/shard_map/all_gather | solution.py:24
  135.3 21.2 %all-gather.3 = f32[16,1,10]{2,1,0:T(1,128)} all-gather(f32[1,1,10]{2,1,0:T(1,128)S(1)} %bitcast.277), channel_id=1, replica_groups=mesh['seq'=16,'head'=8,'dp'=2] {'seq'}, dimensions={0}, use_global_device_ids=true | all-gather | bytes 680 | tf_op jit(solution)/shard_map/all_gather | solution.py:48
  158.4 1.8 reshape.371
  160.3 1.8 reshape.373
  162.1 22.0 %while.21 = (s32[]{:T(128)}, f32[10,128,64]{2,1,0:T(8,128)S(1)}, s32[]{:T(128)}, bf16[16,10]{1,0:T(8,128)(2,1)S(1)}, bf16[16,10,128,64]{2,3,1,0:T(8,128)(2,1)}, /*index=5*/s32[]{:T(128)}, s32[]{:T(128)}) while((s32[]{:T(128)}, f32[10,128,64]{2,1,0:T(8,128)S(1)}, s32[]{:T(128)}, bf16[16,10]{1,0:T(8,128)(2,1)S(1)}, ...), condition=%wide.region_3.4_spmd.clone, body=%wide.region_2.3_spmd.clone.sunk | while | flops 409614 | bytes 1474765 | solution.py:41
  184.0 25.6 %all-gather.9.cloned.1.call-done = f32[160,128,64]{1,2,0:T(8,128)} async-done(((f32[10,128,64]{1,2,0:T(8,128)}), f32[160,128,64]{1,2,0:T(8,128)}) %all-gather.9.cloned.1.call-update) | async-done | bytes 5242896 | tf_op jit(solution)/shard_map/all_gather | solution.py:48
  209.7 57.4 %while.20 = (s32[]{:T(128)}, f32[10,128,64]{2,1,0:T(8,128)S(1)}, s32[]{:T(128)}, f32[16,10]{1,0:T(8,128)}, f32[16,10,128,64]{2,3,1,0:T(8,128)}, /*index=5*/s32[]{:T(128)}, s32[]{:T(128)}, s32[]{:T(128)}, s32[]{:T(128)}) while((s32[]{:T(128)}, f32[10,128,64]{2,1,0:T(8,128)S(1)}, s32[]{:T(128)}, f32[16,10]{1,0:T(8,128)}, ...), condition=%wide.region_5.6_spmd, body=%wide.region_4.5_spmd.sunk | while | flops 163846 | bytes 2294027 | solution.py:57
  209.7 1.7 constant_dynamic-slice_fusion.4
  213.6 1.7 constant_dynamic-slice_fusion.4
  217.4 1.7 constant_dynamic-slice_fusion.4
  221.2 1.7 constant_dynamic-slice_fusion.4
  225.0 1.7 constant_dynamic-slice_fusion.4
  228.9 1.7 constant_dynamic-slice_fusion.4
  232.7 1.7 constant_dynamic-slice_fusion.4
  236.5 1.7 constant_dynamic-slice_fusion.4
  240.3 1.7 constant_dynamic-slice_fusion.4
  244.1 1.7 constant_dynamic-slice_fusion.4
  248.0 1.7 constant_dynamic-slice_fusion.4
  251.8 1.7 constant_dynamic-slice_fusion.4
  255.6 1.7 constant_dynamic-slice_fusion.4
  259.4 1.7 constant_dynamic-slice_fusion.4
  263.3 1.7 constant_dynamic-slice_fusion.4
  271.9 2.1 fusion.71
  275.0 3.0 copy.262
  278.1 3.0 copy.251
  281.1 2.2 copy.254
  283.3 2.1 convolution_bitcast_fusion
  285.5 5.8 fusion.19
  291.3 3.9 multiply_reduce_fusion.3
  296.8 1.7 fusion.120
  300.1 2.6 reduce-window.42
  303.1 2.3 broadcast_multiply_fusion
  305.4 1.7 fusion.65
  309.1 7.0 all-to-all-start.5
  317.1 6.8 all-to-all-done.5
  325.2 28.1 %reduce-scatter.4.cloned.1.call-done = bf16[32,256]{1,0:T(8,128)(2,1)} async-done(((bf16[256,256]{1,0:T(8,128)(2,1)}), bf16[32,256]{1,0:T(8,128)(2,1)}) %reduce-scatter.4.cloned.1.call-update) | async-done | bytes 16400
  353.2 2.7 fusion.1
  356.9 3.6 broadcast_multiply_fusion.1
  361.1 6.1 fusion.48
  367.2 2.4 copy.238
  370.9 2.4 copy.252
  374.6 2.5 add_convert_fusion
  377.2 4.4 all-to-all-start.2
  381.8 14.5 %all-to-all-done.2 = bf16[8,32,640]{2,1,0:T(8,128)(2,1)S(1)} async-done(((bf16[8,32,640]{2,1,0:T(8,128)(2,1)}), bf16[8,32,640]{2,1,0:T(8,128)(2,1)S(1)}, u32[]{:S(2)}, u32[]{:S(2)}) %all-to-all-start.2) | async-done | bytes 327712 | tf_op jit(solution)/shard_map/all_to_all | solution.py:198
  396.3 3.4 all-to-all-start.4
  399.9 349.9 %psum.23 = f32[3,80]{1,0:T(4,128)} all-reduce(f32[3,80]{1,0:T(4,128)S(1)} %dynamic_update_slice.19), channel_id=1, replica_groups=mesh['seq'=16,'head'=8,'dp'=2] {'seq','head'}, use_global_device_ids=true, to_apply=%region_25.26 | all-reduce | flops 240 | bytes 1920 | tf_op jit(solution)/shard_map/psum | solution.py:219
  752.7 3.3 copy.269
  (356 shorter events, 106.2 us)
Async XLA Ops:
  7.2 9.0 %copy-start = (bf16[2560,256]{1,0:T(8,128)(2,1)S(1)}, bf16[2560,256]{1,0:T(8,128)(2,1)}, u32[]{:S(2)}) copy-start(bf16[2560,256]{1,0:T(8,128)(2,1)} %param.15) | copy-start | bytes 3932164
  7.2 15.6 %copy-start.16 = (bf16[32,5120]{1,0:T(8,128)(2,1)S(1)}, bf16[32,5120]{1,0:T(8,128)(2,1)}, u32[]{:S(2)}) copy-start(bf16[32,5120]{1,0:T(8,128)(2,1)} %param.14) | copy-start | bytes 983044
  9.5 14.5 %all-to-all-start.1 = ((bf16[8,2,160]{2,1,0:T(2,128)(2,1)}), bf16[8,2,160]{2,1,0:T(2,128)(2,1)S(1)}, u32[]{:S(2)}, u32[]{:S(2)}) async-start(bf16[8,2,160]{2,1,0:T(2,128)(2,1)} %reshape.399), calls=%async_computation.1 | async-start | bytes 16384 | tf_op jit(solution)/shard_map/all_to_all | solution.py:159
  17.4 40.7 %copy-start.20 = (bf16[32,256]{1,0:T(8,128)(2,1)}, bf16[32,256]{1,0:T(8,128)(2,1)S(1)}, u32[]{:S(2)}) copy-start(bf16[32,256]{1,0:T(8,128)(2,1)S(1)} %convolution_convert_fusion) | copy-start | bytes 49156
  17.5 12.0 %collective-permute-start = (bf16[32,256]{1,0:T(8,128)(2,1)S(1)}, bf16[32,256]{1,0:T(8,128)(2,1)S(1)}, u32[]{:S(2)}, u32[]{:S(2)}) collective-permute-start(bf16[32,256]{1,0:T(8,128)(2,1)S(1)} %convolution_convert_fusion), channel_id=1, source_target_pairs={{0,2},{2,4},{4,6},{6,8},{8,10},{10,12},{12,14},{14,0},{1,3},{3,5},... | collective-permute-start | bytes 49160 | tf_op jit(solution)/shard_map/ppermute | solution.py:15
  20.3 37.9 %copy-start.41 = (f32[10]{0:T(128)}, f32[10]{0:T(128)S(1)}, u32[]{:S(2)}) copy-start(f32[10]{0:T(128)S(1)} %fusion.115) | copy-start | bytes 124
  21.0 37.1 %copy-start.43 = (f32[10]{0:T(128)}, f32[10]{0:T(128)S(1)}, u32[]{:S(2)}) copy-start(f32[10]{0:T(128)S(1)} %dynamic_slice.77) | copy-start | bytes 124
  24.0 48.2 %all-to-all-start = ((bf16[32,8,640]{2,0,1:T(8,128)(2,1)}), bf16[32,8,640]{2,0,1:T(8,128)(2,1)}, u32[]{:S(2)}, u32[]{:S(2)}) async-start(bf16[32,8,640]{2,0,1:T(8,128)(2,1)} %bitcast.236), calls=%async_computation | async-start | bytes 655360 | tf_op jit(solution)/shard_map/all_to_all | solution.py:158
  29.3 28.8 %copy-start.17 = (bf16[8,10,32]{2,1,0:T(8,128)(2,1)}, bf16[8,10,32]{2,1,0:T(8,128)(2,1)S(1)}, u32[]{:S(2)}) copy-start(bf16[8,10,32]{2,1,0:T(8,128)(2,1)S(1)} %reshape.400) | copy-start | bytes 15364
  29.5 28.7 %copy-start.24 = (f32[256,10]{0,1:T(8,128)}, f32[256,10]{0,1:T(8,128)S(1)}, u32[]{:S(2)}) copy-start(f32[256,10]{0,1:T(8,128)S(1)} %reshape.372) | copy-start | bytes 30724
  29.5 28.7 %copy-start.31 = (bf16[32,256]{1,0:T(8,128)(2,1)}, bf16[32,256]{1,0:T(8,128)(2,1)S(1)}, u32[]{:S(2)}) copy-start(bf16[32,256]{1,0:T(8,128)(2,1)S(1)} %collective-permute-done) | copy-start | bytes 49156
  29.5 8.2 %collective-permute-start.1 = (bf16[32,256]{1,0:T(8,128)(2,1)S(1)}, bf16[32,256]{1,0:T(8,128)(2,1)S(1)}, u32[]{:S(2)}, u32[]{:S(2)}) collective-permute-start(bf16[32,256]{1,0:T(8,128)(2,1)S(1)} %collective-permute-done), channel_id=1, source_target_pairs={{0,2},{2,4},{4,6},{6,8},{8,10},{10,12},{12,14},{14,0},{1,3},{3,5},... | collective-permute-start | bytes 49160 | tf_op jit(solution)/shard_map/ppermute | solution.py:15
  37.7 14.9 %copy-start.32 = (bf16[32,256]{1,0:T(8,128)(2,1)}, bf16[32,256]{1,0:T(8,128)(2,1)S(1)}, u32[]{:S(2)}) copy-start(bf16[32,256]{1,0:T(8,128)(2,1)S(1)} %collective-permute-done.1) | copy-start | bytes 49156
  37.7 4.9 collective-permute-start.2
  42.7 15.5 %copy-start.33 = (bf16[32,256]{1,0:T(8,128)(2,1)}, bf16[32,256]{1,0:T(8,128)(2,1)S(1)}, u32[]{:S(2)}) copy-start(bf16[32,256]{1,0:T(8,128)(2,1)S(1)} %collective-permute-done.2) | copy-start | bytes 49156
  42.7 4.9 collective-permute-start.3
  42.8 15.4 %copy-start.21 = (f32[2,8,2,128]{3,1,2,0:T(8,128)}, f32[2,8,2,128]{3,1,2,0:T(8,128)S(1)}, u32[]{:S(2)}) copy-start(f32[2,8,2,128]{3,1,2,0:T(8,128)S(1)} %copy.285) | copy-start | bytes 49156
  47.6 10.6 %copy-start.34 = (bf16[32,256]{1,0:T(8,128)(2,1)}, bf16[32,256]{1,0:T(8,128)(2,1)S(1)}, u32[]{:S(2)}) copy-start(bf16[32,256]{1,0:T(8,128)(2,1)S(1)} %collective-permute-done.3) | copy-start | bytes 49156
  47.6 4.9 collective-permute-start.4
  52.6 5.6 copy-start.35
  52.6 5.1 collective-permute-start.5
  53.3 5.0 copy-start.28
  57.6 7.4 collective-permute-start.6
  63.1 8.4 %copy-start.7 = (f32[256,10]{1,0:T(8,128)}, f32[256,10]{1,0:T(8,128)S(1)}, u32[]{:S(2)}) copy-start(f32[256,10]{1,0:T(8,128)S(1)} %copy.230) | copy-start | bytes 30724
  72.2 17.9 %all-to-all-start.3 = ((bf16[32,8,640]{2,0,1:T(8,128)(2,1)}), bf16[32,8,640]{2,0,1:T(8,128)(2,1)S(1)}, u32[]{:S(2)}, u32[]{:S(2)}) async-start(bf16[32,8,640]{2,0,1:T(8,128)(2,1)} %bitcast.251), calls=%async_computation.3 | async-start | bytes 655360 | tf_op jit(solution)/shard_map/all_to_all | solution.py:160
  78.9 83.1 %all-gather.7.cloned.1.call-start = ((), (), s32[]{:S(2)}) async-start(), calls=%async_computation.7 | async-start | bytes 2785280 | tf_op jit(solution)/shard_map/all_gather | solution.py:24
  83.3 10.3 %copy-start.10 = (bf16[512,256]{1,0:T(8,128)(2,1)}, bf16[512,256]{1,0:T(8,128)(2,1)S(1)}, u32[]{:S(2)}) copy-start(bf16[512,256]{1,0:T(8,128)(2,1)S(1)} %constant_dynamic-update-slice_fusion) | copy-start | bytes 786436
  83.3 11.9 %copy-start.49 = (f32[10]{0:T(128)S(1)}, f32[10]{0:T(128)}, u32[]{:S(2)}) copy-start(f32[10]{0:T(128)} %exponential_multiply_fusion) | copy-start | bytes 124
  90.1 3.5 copy-start.1
  98.0 16.1 %copy-start.22 = (f32[2,8,2,128]{3,1,2,0:T(8,128)S(1)}, f32[2,8,2,128]{3,1,2,0:T(8,128)}, u32[]{:S(2)}) copy-start(f32[2,8,2,128]{3,1,2,0:T(8,128)} %copy-done.21) | copy-start | bytes 49156
  98.0 37.3 %copy-start.48 = (f32[10]{0:T(128)S(1)}, f32[10]{0:T(128)}, u32[]{:S(2)}) copy-start(f32[10]{0:T(128)} %get-tuple-element.506) | copy-start | bytes 124
  98.0 111.6 %all-gather.9.cloned.1.call-start = ((), (), s32[]{:S(2)}) async-start(), calls=%async_computation.8 | async-start | bytes 5570560 | tf_op jit(solution)/shard_map/all_gather | solution.py:48
  113.4 46.8 %copy-start.2 = (bf16[32,8,640]{2,0,1:T(8,128)(2,1)S(1)}, bf16[32,8,640]{2,0,1:T(8,128)(2,1)}, u32[]{:S(2)}) copy-start(bf16[32,8,640]{2,0,1:T(8,128)(2,1)} %copy-done.1) | copy-start | bytes 983044
  157.3 116.6 %copy-start.4 = (f32[256,128]{1,0:T(8,128)}, f32[256,128]{1,0:T(8,128)S(1)}, u32[]{:S(2)}) copy-start(f32[256,128]{1,0:T(8,128)S(1)} %get-tuple-element.362) | copy-start | bytes 393220
  268.8 9.3 %copy-start.45 = (f32[10]{0:T(128)}, f32[10]{0:T(128)S(1)}, u32[]{:S(2)}) copy-start(f32[10]{0:T(128)S(1)} %slice_bitcast_fusion) | copy-start | bytes 124
  285.4 5.8 copy-start.13
  285.5 5.8 copy-start.14
  285.5 5.8 copy-start.19
  285.5 5.8 copy-start.27
  285.5 5.8 copy-start.30
  285.5 5.8 copy-start.39
  295.2 4.6 copy-start.38
  295.2 4.7 copy-start.37
  295.2 4.8 copy-start.47
  295.2 4.8 copy-start.46
  303.0 4.1 copy-start.9
  303.1 4.1 copy-start.15
  303.1 4.5 copy-start.5
  305.4 2.9 copy-start.18
  305.4 18.6 %copy-start.3 = (bf16[32,2560]{1,0:T(8,128)(2,1)S(1)}, bf16[32,2560]{1,0:T(8,128)(2,1)}, u32[]{:S(2)}) copy-start(bf16[32,2560]{1,0:T(8,128)(2,1)} %param.12) | copy-start | bytes 491524
  309.1 14.7 %all-to-all-start.5 = ((bf16[8,2,160]{2,1,0:T(2,128)(2,1)}), bf16[8,2,160]{2,1,0:T(2,128)(2,1)S(1)}, u32[]{:S(2)}, u32[]{:S(2)}) async-start(bf16[8,2,160]{2,1,0:T(2,128)(2,1)} %reshape.401), calls=%async_computation.5 | async-start | bytes 16384 | tf_op jit(solution)/shard_map/all_to_all | solution.py:200
  316.2 37.1 %reduce-scatter.4.cloned.1.call-start = ((), (), s32[]{:S(2)}) async-start(), calls=%async_computation.9 | async-start | bytes 147456
  317.0 435.7 %all-reduce.4.cloned.1.call-start = ((), (), s32[]{:S(2)}) async-start(), calls=%async_computation.10 | async-start | bytes 6881280 | tf_op jit(solution)/shard_map/psum | solution.py:219
  325.2 30.8 %copy-start.51 = (f32[80]{0:T(128)S(1)}, f32[80]{0:T(128)}, u32[]{:S(2)}) copy-start(f32[80]{0:T(128)} %param.19) | copy-start | bytes 964
  325.2 31.1 %copy-start.11 = (bf16[512,256]{1,0:T(8,128)(2,1)S(1)}, bf16[512,256]{1,0:T(8,128)(2,1)}, u32[]{:S(2)}) copy-start(bf16[512,256]{1,0:T(8,128)(2,1)} %copy-done.10) | copy-start | bytes 786436
  356.9 4.3 copy-start.23
  356.9 4.3 copy-start.29
  373.3 8.3 %copy-start.36 = (f32[640]{0:T(1024)S(1)}, f32[640]{0:T(1024)}, u32[]{:S(2)}) copy-start(f32[640]{0:T(1024)} %get-tuple-element.533) | copy-start | bytes 7684
  373.3 8.4 %copy-start.50 = (f32[80]{0:T(128)S(1)}, f32[80]{0:T(128)}, u32[]{:S(2)}) copy-start(f32[80]{0:T(128)} %param.18) | copy-start | bytes 964
  374.6 375.2 %copy-start.26 = (bf16[32,256]{1,0:T(8,128)(2,1)S(1)}, bf16[32,256]{1,0:T(8,128)(2,1)}, u32[]{:S(2)}) copy-start(bf16[32,256]{1,0:T(8,128)(2,1)} %reduce-scatter.4.cloned.1.call-done) | copy-start | bytes 49156
  374.6 375.7 %copy-start.6 = (bf16[2560,80]{0,1:T(8,128)(2,1)S(1)}, bf16[2560,80]{0,1:T(8,128)(2,1)}, u32[]{:S(2)}) copy-start(bf16[2560,80]{0,1:T(8,128)(2,1)} %param.16) | copy-start | bytes 1228804
  377.2 19.1 %all-to-all-start.2 = ((bf16[8,32,640]{2,1,0:T(8,128)(2,1)}), bf16[8,32,640]{2,1,0:T(8,128)(2,1)S(1)}, u32[]{:S(2)}, u32[]{:S(2)}) async-start(bf16[8,32,640]{2,1,0:T(8,128)(2,1)} %get-tuple-element.546), calls=%async_computation.2 | async-start | bytes 655360 | tf_op jit(solution)/shard_map/all_to_all | solution.py:198
  396.3 355.7 %all-to-all-start.4 = ((bf16[8,32,640]{2,1,0:T(8,128)(2,1)}), bf16[8,32,640]{2,1,0:T(8,128)(2,1)S(1)}, u32[]{:S(2)}, u32[]{:S(2)}) async-start(bf16[8,32,640]{2,1,0:T(8,128)(2,1)} %get-tuple-element.545), calls=%async_computation.4 | async-start | bytes 655360 | tf_op jit(solution)/shard_map/all_to_all | solution.py:199
  752.7 3.3 copy-start.12
  (5 other events, 11.5 us)
Sparse Core Ops, SparseCore 0:
  98.2 47.6 all-gather.6
  148.9 60.7 all-gather.8
  320.1 33.1 reduce-scatter.3
  360.2 238.0 all-reduce.3
